TPU v7x, 32 devices: a whole 2x2x4 slice. The times are simulated.
32 devices in a mesh: groups: 2 (over x), rows: 8 (over z, y), cols: 2 (over core).
Axes of the slice: x: 2, y: 2, z: 4, core: 2. Of those that a mesh axis runs over, the one named last changes fastest.
Arguments:
- train_emb: bfloat16 [32768, 768], P(('groups', 'rows')), parts along dimension 0
- val_emb: bfloat16 [4, 2048, 768], P(('groups', 'cols')), parts along dimension 0
- tiles: int32 [64, 2, 2], P(('groups', 'rows'), 'cols'), parts along dimension 0, may hold values from 0 to 3, as said below
- counts: int32 [64], P(('groups', 'rows')), parts along dimension 0, may hold values from 1 to 512, 12288 in all
Outputs:
- pot_train: float32 [32768], P(('groups', 'rows')), parts along dimension 0
- pot_val: float32 [4, 2048], P(('groups', 'cols')), parts along dimension 0
- grad_train: bfloat16 [32768, 768], P(('groups', 'rows'), 'cols'), parts along dimension 0
- grad_val: float32 [4, 2048, 768], P(('groups', 'cols'), 'rows'), parts along dimension 0
There are 2 independent parts, one for each index of `groups`. A program takes and returns all parts, laid end to end along the dimension named above; each array names one. Nothing has to cross between parts.
Inputs may be any that keep to these rules, and one draw needn't show every extreme that they name: `tiles`: local validation block index within the column half; the 2 entries of one training block and half differ, and every validation block is paired with some training block in every draw. The counts sum to 12288; some block is full.
All inputs are finite; a program needn't handle non-finite values.
Results may differ from a plain program's by a relative error of at most 0.0029.
Values sent between devices are 32-bit elements; how exact they have to be, the bound alone decides.
A program may use at most 128 MiB of HBM per device.

v0:
```python
import jax
import jax.numpy as jnp
from jax import lax
from jax.sharding import PartitionSpec as P

BLOCK = 512
ITERS = 3


entropy_weight = 0.1
floor_value = -1e30


def merge_train(row_top, row_total):
    joined = lax.pmax(row_top, "cols")
    return (joined, lax.psum(row_total * jnp.exp(row_top - joined), "cols"))


def merge_val(val_top, val_sum):
    joined = lax.pmax(val_top, "rows")
    return (joined, lax.psum(val_sum * jnp.exp(val_top - joined), "rows"))


def body(train_emb, val_emb, tiles, counts):
    feature_width = train_emb.shape[1]
    local_blocks = counts.shape[0]
    row_devices = lax.axis_size("rows")
    col_devices = lax.axis_size("cols")
    live_total = local_blocks * row_devices * (3 * BLOCK // 4)
    val_total = val_emb.shape[1] * col_devices
    train_rows = train_emb.reshape(local_blocks, BLOCK, feature_width)
    val_blocks = val_emb.reshape(-1, BLOCK, feature_width)
    val_local = val_blocks.shape[0]
    picked = tiles.reshape(local_blocks, -1)
    live_rows = jnp.arange(BLOCK, dtype=jnp.int32)[None, :] < counts[:, None]
    live_mask = live_rows[:, None, :, None]
    chosen = val_blocks[picked]
    train_sq = jnp.sum(jnp.square(train_rows.astype(jnp.float32)), axis=-1)
    val_sq = jnp.sum(jnp.square(val_blocks.astype(jnp.float32)), axis=-1)
    inner_prod = jnp.einsum(
        "tid,tkjd->tkij", train_rows, chosen, preferred_element_type=jnp.float32
    )
    cost_tiles = train_sq[:, None, :, None] + val_sq[picked][:, :, None, :] - 2.0 * inner_prod
    block_hot = (picked[..., None] == jnp.arange(val_local, dtype=jnp.int32)).astype(jnp.float32)
    pot_val = jnp.zeros((val_local, BLOCK), jnp.float32)
    pot_train = jnp.zeros((local_blocks, BLOCK), jnp.float32)
    for sweep_index in range(ITERS):
        val_near = pot_val[picked]
        scores = (val_near[:, :, None, :] - cost_tiles) / entropy_weight
        row_top = jnp.max(scores, axis=(1, 3))
        row_total = jnp.sum(jnp.exp(scores - row_top[:, None, :, None]), axis=(1, 3))
        row_top, row_total = merge_train(row_top, row_total)
        pot_train = jnp.where(
            live_rows,
            -entropy_weight * (row_top + jnp.log(row_total))
            + entropy_weight * jnp.log(1.0 / live_total),
            0.0,
        )
        back_scores = jnp.where(
            live_mask, (pot_train[:, None, :, None] - cost_tiles) / entropy_weight, floor_value
        )
        tile_top = jnp.max(back_scores, axis=2)
        val_top = jnp.max(
            jnp.where(block_hot[..., None] > 0, tile_top[:, :, None, :], floor_value), axis=(0, 1)
        )
        tile_sum = jnp.sum(jnp.exp(back_scores - val_top[picked][:, :, None, :]), axis=2)
        val_sum = jnp.einsum("tkv,tkj->vj", block_hot, tile_sum, precision=lax.Precision.HIGHEST)
        val_top, val_sum = merge_val(val_top, val_sum)
        pot_val = -entropy_weight * (val_top + jnp.log(val_sum)) + entropy_weight * jnp.log(
            1.0 / val_total
        )
    transport = jnp.where(
        live_mask,
        jnp.exp(
            (pot_train[:, None, :, None] + pot_val[picked][:, :, None, :] - cost_tiles)
            / entropy_weight
        ),
        0.0,
    )
    row_mass = jnp.sum(transport, axis=(1, 3))
    plan_rounded = transport.astype(jnp.bfloat16)
    pulled = jnp.einsum("tkij,tkjd->tid", plan_rounded, chosen, preferred_element_type=jnp.float32)
    train_terms = (row_mass[..., None] * train_rows.astype(jnp.float32) - pulled).reshape(
        -1, feature_width
    )
    train_half = lax.psum_scatter(train_terms, "cols", scatter_dimension=1, tiled=True)
    grad_train = (live_total * 2.0 * train_half).astype(jnp.bfloat16)
    pushed = jnp.einsum(
        "tkij,tid->tkjd", plan_rounded, train_rows, preferred_element_type=jnp.float32
    )
    val_terms = jnp.einsum(
        "tkv,tkjd->vjd", block_hot, pushed, precision=lax.Precision.HIGHEST
    ).reshape(-1, feature_width)
    share_rows = val_terms.shape[0] // row_devices
    summed = lax.psum(val_terms, "rows")
    owned = lax.dynamic_slice_in_dim(summed, lax.axis_index("rows") * share_rows, share_rows, 0)
    own_val = lax.dynamic_slice_in_dim(
        val_emb[0], lax.axis_index("rows") * share_rows, share_rows, 0
    )
    grad_val = (2.0 * (own_val.astype(jnp.float32) - val_total * owned))[None]
    return (pot_train.reshape(-1), pot_val.reshape(1, -1), grad_train, grad_val)


def solution(mesh):
    return jax.shard_map(
        body,
        mesh=mesh,
        in_specs=(
            P(("groups", "rows"), None),
            P(("groups", "cols"), None, None),
            P(("groups", "rows"), "cols", None),
            P(("groups", "rows")),
        ),
        out_specs=(
            P(("groups", "rows")),
            P(("groups", "cols"), None),
            P(("groups", "rows"), "cols"),
            P(("groups", "cols"), "rows", None),
        ),
        check_vma=False,
    )
```

profile of v0, /device:TPU:11, one launch (start us, length us, event | category | flops | bytes accessed | tf_op | source)
XLA Modules:
  0.0 457.1 jit_solution(12825765720338544950)
XLA Ops:
  9.7 2.6 multiply_reduce_fusion
  12.2 5.4 %gather_fusion.2 = bf16[8,512,768]{2,1,0:T(8,128)(2,1)} fusion(bf16[4,512,768]{2,1,0:T(8,128)(2,1)} %bitcast.51, s32[1024]{0:T(1024)S(1)} %pad_clamp_fusion), kind=kCustom, calls=%fused_computation.2 | custom fusion | bytes 12582944 | tf_op jit(solution)/shard_map/gather | solution.py:37
  19.0 8.0 %fusion.2 = (f32[4,512]{1,0:T(4,128)S(1)}, f32[4,2,512,512]{2,3,1,0:T(8,128)}) fusion(f32[4,2,512]{2,1,0:T(2,128)S(1)} %reshape.117, bf16[4,2,512,768]{3,2,1,0:T(8,128)(2,1)} %bitcast.54, bf16[4,512,768,1]{2,1,3,0:T(8,128)(2,1)S(1)} %bitcast.57, f32[4,2,512]{2,1,0:T(2,128)S(1)} %reshape.125, f32[4,512]{1,0:T(4,128)S(1)} %add.101), kind=kOutput, calls=%fused_computation.25 | convolution fusion | flops 3233806336 | bytes 17874944 | tf_op jit(solution)/shard_map/tid,tkjd->tkij/dot_general | solution.py:40
  26.9 2.8 pmax.42
  29.7 4.4 exponential_reduce_fusion.5
  34.1 2.5 psum.49
  36.9 4.6 fusion.5
  41.6 15.4 %pmax.43 = f32[4,512]{1,0:T(4,128)S(1)} all-reduce(f32[4,512]{1,0:T(4,128)S(1)} %select_reduce_fusion.2), channel_id=1, replica_groups=mesh['groups'=2,'rows'=8,'cols'=2] {'rows'}, use_global_device_ids=true, to_apply=%region_8.9 | all-reduce | flops 2048 | bytes 16384 | tf_op jit(solution)/shard_map/pmax | solution.py:20
  57.6 4.6 %exponential_reduce_fusion.4 = f32[4,2,512]{2,1,0:T(2,128)S(1)} fusion(f32[4,2,512,512]{2,3,1,0:T(8,128)} %get-tuple-element.5, f32[4,2,512]{2,1,0:T(2,128)S(1)} %reshape.141, f32[4,512]{1,0:T(4,128)S(1)} %add_select_fusion.2, pred[4,512]{1,0:T(4,128)(4,1)S(1)} %iota_compare_fusion), kind=kLoop, calls=%fused_computation.21 | loop fusion | flops 10481664 | bytes 8431616 | tf_op jit(solution)/shard_map/reduce_sum | solution.py:66
  62.4 13.9 %psum.50 = f32[4,512]{1,0:T(4,128)S(1)} all-reduce(f32[4,512]{1,0:T(4,128)S(1)} %fusion.13), channel_id=1, replica_groups=mesh['groups'=2,'rows'=8,'cols'=2] {'rows'}, use_global_device_ids=true, to_apply=%region_10.11 | all-reduce | flops 2048 | bytes 16384 | tf_op jit(solution)/shard_map/psum | solution.py:21
  76.9 4.0 fusion.3
  80.9 9.8 %pmax.44 = f32[4,512]{1,0:T(4,128)S(1)} all-reduce(f32[4,512]{1,0:T(4,128)S(1)} %fusion.3), channel_id=1, replica_groups=mesh['groups'=2,'rows'=8,'cols'=2] {'cols'}, use_global_device_ids=true, to_apply=%region_12.13 | all-reduce | flops 2048 | bytes 16384 | tf_op jit(solution)/shard_map/pmax | solution.py:15
  90.6 4.4 exponential_reduce_fusion.3
  97.6 4.6 fusion.6
  102.3 15.9 %pmax.45 = f32[4,512]{1,0:T(4,128)S(1)} all-reduce(f32[4,512]{1,0:T(4,128)S(1)} %select_reduce_fusion.1), channel_id=1, replica_groups=mesh['groups'=2,'rows'=8,'cols'=2] {'rows'}, use_global_device_ids=true, to_apply=%region_17.18 | all-reduce | flops 2048 | bytes 16384 | tf_op jit(solution)/shard_map/pmax | solution.py:20
  118.7 4.6 %exponential_reduce_fusion.2 = f32[4,2,512]{2,1,0:T(2,128)S(1)} fusion(f32[4,2,512,512]{2,3,1,0:T(8,128)} %get-tuple-element.5, f32[4,2,512]{2,1,0:T(2,128)S(1)} %reshape.157, f32[4,512]{1,0:T(4,128)S(1)} %add_select_fusion.1, pred[4,512]{1,0:T(4,128)(4,1)S(1)} %iota_compare_fusion), kind=kLoop, calls=%fused_computation.17 | loop fusion | flops 10481664 | bytes 8431616 | tf_op jit(solution)/shard_map/reduce_sum | solution.py:66
  123.6 13.9 %psum.52 = f32[4,512]{1,0:T(4,128)S(1)} all-reduce(f32[4,512]{1,0:T(4,128)S(1)} %fusion.14), channel_id=1, replica_groups=mesh['groups'=2,'rows'=8,'cols'=2] {'rows'}, use_global_device_ids=true, to_apply=%region_19.20 | all-reduce | flops 2048 | bytes 16384 | tf_op jit(solution)/shard_map/psum | solution.py:21
  138.1 4.0 fusion.4
  142.1 9.6 %pmax.46 = f32[4,512]{1,0:T(4,128)S(1)} all-reduce(f32[4,512]{1,0:T(4,128)S(1)} %fusion.4), channel_id=1, replica_groups=mesh['groups'=2,'rows'=8,'cols'=2] {'cols'}, use_global_device_ids=true, to_apply=%region_21.22 | all-reduce | flops 2048 | bytes 16384 | tf_op jit(solution)/shard_map/pmax | solution.py:15
  151.7 4.4 exponential_reduce_fusion.1
  156.1 2.5 psum.53
  158.7 4.6 %fusion.7 = f32[4,2,512]{2,1,0:T(2,128)S(1)} fusion(f32[4,2,512,512]{2,3,1,0:T(8,128)} %get-tuple-element.5, f32[4,512]{1,0:T(4,128)S(1)} %add_select_fusion, pred[4,512]{1,0:T(4,128)(4,1)S(1)} %iota_compare_fusion), kind=kLoop, calls=%fused_computation.30 | loop fusion | flops 8384512 | bytes 8415232 | tf_op jit(solution)/shard_map/reduce_max | solution.py:62
  163.4 15.7 %pmax.47 = f32[4,512]{1,0:T(4,128)S(1)} all-reduce(f32[4,512]{1,0:T(4,128)S(1)} %select_reduce_fusion), channel_id=1, replica_groups=mesh['groups'=2,'rows'=8,'cols'=2] {'rows'}, use_global_device_ids=true, to_apply=%region_26.27 | all-reduce | flops 2048 | bytes 16384 | tf_op jit(solution)/shard_map/pmax | solution.py:20
  179.7 4.6 %exponential_reduce_fusion = f32[4,2,512]{2,1,0:T(2,128)S(1)} fusion(f32[4,2,512,512]{2,3,1,0:T(8,128)} %get-tuple-element.5, f32[4,2,512]{2,1,0:T(2,128)S(1)} %reshape.173, f32[4,512]{1,0:T(4,128)S(1)} %add_select_fusion, pred[4,512]{1,0:T(4,128)(4,1)S(1)} %iota_compare_fusion), kind=kLoop, calls=%fused_computation.13 | loop fusion | flops 10481664 | bytes 8431616 | tf_op jit(solution)/shard_map/reduce_sum | solution.py:66
  184.5 14.2 %psum.54 = f32[4,512]{1,0:T(4,128)S(1)} all-reduce(f32[4,512]{1,0:T(4,128)S(1)} %fusion.15), channel_id=1, replica_groups=mesh['groups'=2,'rows'=8,'cols'=2] {'rows'}, use_global_device_ids=true, to_apply=%region_28.29 | all-reduce | flops 2048 | bytes 16384 | tf_op jit(solution)/shard_map/psum | solution.py:21
  199.3 7.0 %fusion.27 = f32[4,2,512,768]{3,2,1,0:T(8,128)S(1)} fusion(bf16[4,512,768,1]{2,1,3,0:T(8,128)(2,1)} %bitcast.56, f32[4,2,512,512]{2,3,1,0:T(8,128)} %get-tuple-element.5, f32[4,2,512]{2,1,0:T(2,128)S(1)} %reshape.181, f32[4,512]{1,0:T(4,128)S(1)} %add_select_fusion, pred[4,512]{1,0:T(4,128)(4,1)S(1)} %iota_compare_fusion), kind=kOutput, calls=%fused_computation.72 | convolution fusion | flops 3231711232 | bytes 24143872 | tf_op jit(solution)/shard_map/tkij,tid->tkjd/dot_general | solution.py:88
  206.3 16.0 %fusion.10 = f32[4,512,768]{2,0,1:T(4,128)S(1)} fusion(f32[4,2,512,768]{3,2,1,0:T(8,128)S(1)} %fusion.27, s32[4,2]{0,1:T(2,128)S(1)} %bitcast.65), kind=kOutput, calls=%fused_computation.37 | convolution fusion | flops 150994976 | bytes 18874400 | tf_op jit(solution)/shard_map/tkv,tkjd->vjd/dot_general | solution.py:91
  222.3 3.8 copy.30
  226.5 4.7 %fusion.9 = f32[4,512]{1,0:T(4,128)S(1)} fusion(f32[4,2,512,512]{2,3,1,0:T(8,128)} %get-tuple-element.5, f32[4,2,512]{2,1,0:T(2,128)S(1)} %reshape.181, f32[4,512]{1,0:T(4,128)S(1)} %add_select_fusion, pred[4,512]{1,0:T(4,128)(4,1)S(1)} %iota_compare_fusion), kind=kLoop, calls=%fused_computation.35 | loop fusion | flops 10483712 | bytes 8423424 | tf_op jit(solution)/shard_map/reduce_sum | solution.py:80
  231.2 12.1 %bitcast_subtract_fusion.1 = f32[4,512,768]{2,1,0:T(8,128)} fusion(bf16[4,512,768]{2,1,0:T(8,128)(2,1)S(1)} %bitcast.58, f32[4,512]{1,0:T(4,128)S(1)} %fusion.9, bf16[4,2,512,768]{3,2,1,0:T(8,128)(2,1)} %bitcast.55, f32[4,2,512,512]{2,3,1,0:T(8,128)} %get-tuple-element.5, f32[4,2,512]{2,1,0:T(2,128)S(1)} %reshape.181, f32[4,512]{1,0:T(4,128)S(1)} %add_select_fusion, ...), kind=kOutput, calls=%fused_computation.31 | convolution fusion | flops 3236429824 | bytes 24152064 | tf_op jit(solution)/shard_map/tkij,tkjd->tid/dot_general | solution.py:82
  244.5 199.7 %all-reduce.2.cloned.1.call-done = f32[2048,768]{1,0:T(8,128)} async-done(((f32[2048,768]{1,0:T(8,128)}), f32[2048,768]{1,0:T(8,128)}) %all-reduce.2.cloned.1.call-update) | async-done | bytes 6291472 | tf_op jit(solution)/shard_map/psum | solution.py:95
  446.4 3.3 multiply_convert_fusion
  (59 shorter events, 14.0 us)
Async XLA Ops:
  8.0 10.3 %copy-start = (bf16[2048,768]{1,0:T(8,128)(2,1)S(1)}, bf16[2048,768]{1,0:T(8,128)(2,1)}, u32[]{:S(2)}) copy-start(bf16[2048,768]{1,0:T(8,128)(2,1)} %param.4) | copy-start | bytes 9437188
  8.0 436.2 %all-reduce.2.cloned.1.call-start = ((), (), s32[]{:S(2)}) async-start(), calls=%async_computation.2 | async-start | bytes 12582912 | tf_op jit(solution)/shard_map/psum | solution.py:95
  26.9 9.7 %copy-start.3 = (s32[4]{0:T(128)S(1)}, s32[4]{0:T(128)}, u32[]{:S(2)}) copy-start(s32[4]{0:T(128)} %param.7) | copy-start | bytes 52
  26.9 9.9 %copy-start.2 = (s32[4,1,2]{0,2,1:T(2,128)S(1)}, s32[4,1,2]{0,2,1:T(2,128)}, u32[]{:S(2)}) copy-start(s32[4,1,2]{0,2,1:T(2,128)} %param.6) | copy-start | bytes 100
  226.1 5.0 %copy-start.1 = (bf16[2048,768]{1,0:T(8,128)(2,1)S(1)}, bf16[2048,768]{1,0:T(8,128)(2,1)}, u32[]{:S(2)}) copy-start(bf16[2048,768]{1,0:T(8,128)(2,1)} %param.4) | copy-start | bytes 9437188
  226.2 220.2 %reduce-scatter.2.cloned.1.call-start = ((), (), s32[]{:S(2)}) async-start(), calls=%async_computation.1 | async-start | bytes 9437184 | tf_op jit(solution)/shard_map/reduce_scatter | solution.py:86
Sparse Core Ops, SparseCore 0:
  226.3 217.8 all-reduce.1
Sparse Core Ops, SparseCore 1:
  243.4 24.0 reduce-scatter.1
where the time goes:
time: 461 us; the launch traced here: 457 us
  waiting for transfers between devices  200 us (43%)
  blocking collectives  119 us (26%)
  other arithmetic  63.6 us (14%)
  matrix products  43.7 us (9%)
  between operations  15.8 us (3%)
  local copies, waits for them, and re-layouts  15.4 us (3%)
    psum x1, waiting for transfers between devices, body(): summed = lax.psum(val_terms, 'rows')  200 us
    pmax x3, blocking collectives, merge_val(): joined = lax.pmax(val_top, 'rows')  46.9 us
    psum x3, blocking collectives, merge_val(): return (joined, lax.psum(val_sum * jnp.exp(val_top - joined), 'rows'))  42 us
    pmax x3, blocking collectives, merge_train(): joined = lax.pmax(row_top, 'cols')  22.2 us
    dot_general x1, matrix products, body(): jnp.einsum('tkv,tkjd->vjd', block_hot, pushed, precision=lax.Precision.HI...  16 us
    reduce_sum x3, other arithmetic, body(): jnp.sum(jnp.exp(back_scores - val_top[picked][:, :, None, :]), axis=2)  13.9 us
    reduce_max x3, other arithmetic, body(): tile_top = jnp.max(back_scores, axis=2)  13.7 us
    reduce_sum x3, other arithmetic, body(): jnp.sum(jnp.exp(scores - row_top[:, None, :, None]), axis=(1, 3))  13.1 us
  transfers between devices with their start and end apart: 2, of which 1 were waited for; matrix products, arithmetic and copies ran while one was open for 4% of the time, Pallas kernels for 0%

commit v1 on v0

v1 whole, which is shorter than its diff:
```python
import functools
import math

import jax
import jax.numpy as jnp
from jax import lax
from jax.experimental import pallas as pl
from jax.experimental.pallas import tpu as pltpu
from jax.sharding import PartitionSpec as P

BLOCK = 512
ITERS = 3
LANES = 128
WEIGHT = 0.1
SCALE = math.log2(math.e) / WEIGHT
FLOOR = -1e30
MESH = pl.DeviceIdType.MESH
STRIPS = BLOCK // LANES


def strip(index):
    return pl.ds(index * LANES, LANES)


def diagonal():
    return lax.broadcasted_iota(jnp.int32, (LANES, LANES), 0) == lax.broadcasted_iota(
        jnp.int32, (LANES, LANES), 1
    )


def to_row(column):
    return jnp.sum(
        jnp.where(diagonal(), jnp.broadcast_to(column, (LANES, LANES)), 0.0), axis=0, keepdims=True
    )


def to_column(row):
    return jnp.sum(
        jnp.where(diagonal(), jnp.broadcast_to(row, (LANES, LANES)), 0.0), axis=1, keepdims=True
    )


def kernel(
    n, blocks, vals,
    tiles_ref, counts_ref, x_ref, y_ref,
    pot_train_ref, pot_val_ref, grad_train_ref, grad_val_ref,
    cost, plan, chosen, val_sq, g_ref, f_wide, mass_wide, tile_top, tile_sum, row_part,
    row_box, val_box, away, home, paired, landed, term_out, term_in,
    row_send, row_recv, val_send, val_recv, pair_send, pair_recv, own_send, own_recv,
    term_send, term_recv,
):
    me = lax.axis_index("rows")
    core = lax.axis_index("cols")
    other = 1 - core
    width = x_ref.shape[1]
    half_width = width // 2
    live_total = blocks * n * (3 * BLOCK // 4)
    val_total = vals * BLOCK * 2
    pairs = n // 2
    share = vals * BLOCK // n
    stage = lax.div(me, 2)
    side = lax.rem(me, 2)
    mate = stage * 2 + 1 - side

    barrier = pltpu.get_barrier_semaphore()

    @pl.loop(1, n)
    def _(d):
        pl.semaphore_signal(
            barrier, inc=1, device_id={"rows": lax.rem(me + d, n)}, device_id_type=MESH
        )

    pl.semaphore_signal(barrier, inc=1, device_id={"cols": other}, device_id_type=MESH)
    pl.semaphore_wait(barrier, n)

    def pick(q, rows_of, spare):
        found = rows_of(0)
        for v in range(1, vals):
            found = jnp.where(tiles_ref[q][:, 0:spare] == v, rows_of(v), found)
        return found

    def g_of(q):
        return pick(q, lambda v: g_ref[v], BLOCK)

    def block_rows(index):
        return pl.ds(pl.multiple_of(index * BLOCK, BLOCK), BLOCK)

    for v in range(vals):
        for c in range(STRIPS):
            rows = y_ref[pl.ds(v * BLOCK + c * LANES, LANES), :].astype(jnp.float32)
            val_sq[v, :, strip(c)] = to_row(jnp.sum(rows * rows, axis=1, keepdims=True))

    @pl.loop(0, blocks)
    def _(t):
        x = x_ref[block_rows(t), :]
        xf = x.astype(jnp.float32)
        x_sq = jnp.sum(xf * xf, axis=1, keepdims=True)
        for k in range(2):
            q = t * 2 + k
            for j in range(width // LANES):
                chosen[q, :, strip(j)] = pick(
                    q, lambda v: y_ref[v * BLOCK : (v + 1) * BLOCK, strip(j)], LANES
                )
            inner = lax.dot_general(
                x, chosen[q], (((1,), (1,)), ((), ())),
                preferred_element_type=jnp.float32,
            )
            cost[t * 2 + k] = ((x_sq + pick(q, lambda v: val_sq[v], BLOCK)) - 2.0 * inner) * SCALE

    g_ref[...] = jnp.zeros_like(g_ref)

    def val_copy(it, peer, slot):
        return pltpu.make_async_remote_copy(
            src_ref=val_box.at[it, slot], dst_ref=val_box.at[it, slot],
            send_sem=val_send.at[it, peer], recv_sem=val_recv.at[it, slot],
            device_id={"rows": peer}, device_id_type=MESH,
        )

    @pl.loop(0, ITERS)
    def _(it):
        @pl.loop(0, blocks)
        def _(t):
            g = [g_of(t * 2 + k) for k in range(2)]
            for c in range(STRIPS):
                def score(k, j):
                    return g[k][:, j * LANES : (j + 1) * LANES] - cost[t * 2 + k, strip(c), strip(j)]
                top = jnp.full((LANES, LANES), FLOOR, jnp.float32)
                for k in range(2):
                    for j in range(STRIPS):
                        top = jnp.maximum(top, score(k, j))
                top = jnp.max(top, axis=1, keepdims=True)
                wide = jnp.broadcast_to(top, (LANES, LANES))
                total = jnp.zeros((LANES, LANES), jnp.float32)
                for k in range(2):
                    for j in range(STRIPS):
                        total = total + jnp.exp2(score(k, j) - wide)
                total = jnp.sum(total, axis=1, keepdims=True)
                row_part[t, :, strip(c)] = to_row(top)
                row_part[blocks + t, :, strip(c)] = to_row(total)

        for q in range(2 * blocks):
            row_box[it, core, q : q + 1, :] = row_part[q]
        out = pltpu.make_async_remote_copy(
            src_ref=row_box.at[it, core], dst_ref=row_box.at[it, core],
            send_sem=row_send.at[it], recv_sem=row_recv.at[it],
            device_id={"cols": other}, device_id_type=MESH,
        )
        out.start()
        out.wait()
        tops = [row_box[it, q, 0:blocks, :] for q in range(2)]
        top = jnp.maximum(tops[0], tops[1])
        total = sum(
            row_box[it, q, blocks : 2 * blocks, :] * jnp.exp2(tops[q] - top) for q in range(2)
        )
        f_all = math.log2(1.0 / live_total) - (top + jnp.log2(total))
        lane = lax.broadcasted_iota(jnp.int32, (1, BLOCK), 1)
        for t in range(blocks):
            live = lane < counts_ref[t]
            pot_train_ref[t : t + 1, :] = jnp.where(live, f_all[t : t + 1] * (1.0 / SCALE), 0.0)
            f = jnp.where(live, f_all[t : t + 1], FLOOR)
            for c in range(STRIPS):
                f_wide[pl.ds(t * BLOCK + c * LANES, LANES), :] = jnp.broadcast_to(
                    to_column(f[:, c * LANES : (c + 1) * LANES]), (LANES, LANES)
                )

        @pl.loop(0, blocks)
        def _(t):
            for k in range(2):
                for c in range(STRIPS):
                    score = f_wide[block_rows(t), :] - cost[t * 2 + k, :, strip(c)]
                    top = jnp.max(score, axis=0, keepdims=True)
                    total = jnp.sum(jnp.exp2(score - top), axis=0, keepdims=True)
                    tile_top[t * 2 + k, :, strip(c)] = top
                    tile_sum[t * 2 + k, :, strip(c)] = total

        for v in range(vals):
            top = jnp.full((1, BLOCK), FLOOR, jnp.float32)
            for q in range(2 * blocks):
                top = jnp.maximum(top, jnp.where(tiles_ref[q] == v, tile_top[q], FLOOR))
            total = jnp.zeros((1, BLOCK), jnp.float32)
            for q in range(2 * blocks):
                scaled = tile_sum[q] * jnp.exp2(jnp.minimum(tile_top[q] - top, 0.0))
                total = total + jnp.where(tiles_ref[q] == v, scaled, 0.0)
            val_box[it, me, v : v + 1, :] = top
            val_box[it, me, vals + v : vals + v + 1, :] = total

        @pl.loop(1, n)
        def _(d):
            val_copy(it, lax.rem(me + d, n), me).start()

        @pl.loop(1, n)
        def _(d):
            val_copy(it, lax.rem(me + d, n), lax.rem(me + d, n)).wait_recv()

        top = val_box[it, 0, 0:vals, :]
        for q in range(1, n):
            top = jnp.maximum(top, val_box[it, q, 0:vals, :])
        total = jnp.zeros((vals, BLOCK), jnp.float32)
        for q in range(n):
            total = total + val_box[it, q, vals : 2 * vals, :] * jnp.exp2(val_box[it, q, 0:vals, :] - top)
        g = math.log2(1.0 / val_total) - (top + jnp.log2(total))
        pot_val_ref[...] = g * (1.0 / SCALE)
        for v in range(vals):
            g_ref[v] = g[v : v + 1]

    @pl.loop(0, blocks)
    def _(t):
        g = [g_of(t * 2 + k) for k in range(2)]
        for c in range(STRIPS):
            f = f_wide[pl.ds(pl.multiple_of(t * BLOCK + c * LANES, LANES), LANES), :]
            total = jnp.zeros((LANES, LANES), jnp.float32)
            for k in range(2):
                for j in range(STRIPS):
                    value = jnp.exp2(
                        f + g[k][:, j * LANES : (j + 1) * LANES] - cost[t * 2 + k, strip(c), strip(j)]
                    )
                    total = total + value
                    plan[t * 2 + k, strip(c), strip(j)] = value.astype(jnp.bfloat16)
            mass_wide[pl.ds(pl.multiple_of(t * BLOCK + c * LANES, LANES), LANES), :] = (
                jnp.broadcast_to(jnp.sum(total, axis=1, keepdims=True), (LANES, LANES))
            )

    def pair_copy(s):
        return pltpu.make_async_remote_copy(
            src_ref=away.at[s], dst_ref=paired.at[s],
            send_sem=pair_send.at[s], recv_sem=pair_recv.at[s],
            device_id={"rows": mate}, device_id_type=MESH,
        )

    def own_copy(s, slot):
        goal = lax.rem(stage + 1 + s, pairs)
        return pltpu.make_async_remote_copy(
            src_ref=home.at[s], dst_ref=landed.at[slot],
            send_sem=own_send.at[s], recv_sem=own_recv.at[slot],
            device_id={"rows": goal * 2 + side}, device_id_type=MESH,
        )

    def term_copy(t):
        return pltpu.make_async_remote_copy(
            src_ref=term_out.at[t], dst_ref=term_in.at[t],
            send_sem=term_send.at[t], recv_sem=term_recv.at[t],
            device_id={"cols": other}, device_id_type=MESH,
        )

    @pl.loop(0, pairs)
    def _(s):
        goal = lax.rem(stage + 1 + s, pairs)

        def push(which):
            start = (goal * 2 + which) * share
            v = lax.div(start, BLOCK)
            inside = lax.rem(start, BLOCK)
            total = jnp.zeros((share, width), jnp.float32)
            for t in range(blocks):
                if share % LANES == 0:
                    span = pl.ds(pl.multiple_of(inside, share), share)
                    parts = [plan[t * 2 + k, :, span] for k in range(2)]
                    offset = None
                else:
                    base = lax.div(inside, LANES) * LANES
                    span = pl.ds(pl.multiple_of(base, LANES), LANES)
                    parts = [plan[t * 2 + k, :, span] for k in range(2)]
                    offset = inside - base
                zero = jnp.zeros_like(parts[0])
                picked = jnp.where(
                    tiles_ref[t * 2][:, 0 : zero.shape[1]] == v, parts[0],
                    jnp.where(tiles_ref[t * 2 + 1][:, 0 : zero.shape[1]] == v, parts[1], zero),
                )
                product = lax.dot_general(
                    picked, x_ref[t * BLOCK : (t + 1) * BLOCK, :], (((0,), (0,)), ((), ())),
                    preferred_element_type=jnp.float32,
                )
                if offset is not None:
                    keep = product[0:share]
                    for piece in range(1, LANES // share):
                        keep = jnp.where(
                            offset == piece * share, product[piece * share : (piece + 1) * share], keep
                        )
                    product = keep
                total = total + product
            return total

        away[s] = push(1 - side)
        pair_copy(s).start()
        home[s] = push(side)

    @pl.loop(0, blocks)
    def _(t):
        mass = mass_wide[block_rows(t), 0:1]

        def pull(which):
            span = pl.ds(pl.multiple_of(which * half_width, LANES), half_width)
            total = mass * x_ref[block_rows(t), span].astype(jnp.float32)
            pulled = sum(
                jnp.dot(
                    plan[t * 2 + k], chosen[t * 2 + k, :, span],
                    preferred_element_type=jnp.float32,
                )
                for k in range(2)
            )
            return total - pulled

        term_out[t] = pull(other)
        term_copy(t).start()
        cost[t, :, 0:half_width] = pull(core)

    @pl.loop(0, blocks)
    def _(t):
        term_copy(t).wait()
        grad_train_ref[block_rows(t), :] = (
            live_total * 2.0 * (cost[t, :, 0:half_width] + term_in[t])
        ).astype(jnp.bfloat16)

    @pl.loop(0, pairs - 1)
    def _(s):
        pair_copy(s).wait_recv()
        home[s] = home[s] + paired[s]
        own_copy(s, stage).start()

    pair_copy(pairs - 1).wait_recv()
    home[pairs - 1] = home[pairs - 1] + paired[pairs - 1]

    @pl.loop(0, pairs - 1)
    def _(s):
        slot = lax.rem(stage + 1 + s, pairs)
        own_copy(s, slot).wait_recv()
        home[pairs - 1] = home[pairs - 1] + landed[slot]

    own_rows = y_ref[pl.ds(pl.multiple_of(me * share, share), share), :].astype(jnp.float32)
    grad_val_ref[...] = 2.0 * (own_rows - val_total * home[pairs - 1])

    @pl.loop(0, pairs)
    def _(s):
        pair_copy(s).wait_send()

    @pl.loop(0, pairs - 1)
    def _(s):
        own_copy(s, stage).wait_send()

    @pl.loop(0, ITERS)
    def _(it):
        @pl.loop(1, n)
        def _(d):
            val_copy(it, lax.rem(me + d, n), me).wait_send()


def body(train_emb, val_emb, tiles, counts):
    n = lax.axis_size("rows")
    rows, width = train_emb.shape
    blocks = counts.shape[0]
    val_rows = val_emb.shape[1]
    vals = val_rows // BLOCK
    share = val_rows // n
    pairs = n // 2
    half = width // 2
    f32, bf16 = jnp.float32, jnp.bfloat16
    dma = pltpu.SemaphoreType.DMA
    vmem = pl.BlockSpec(memory_space=pltpu.VMEM)
    pot_train, pot_val, grad_train, grad_val = pl.pallas_call(
        functools.partial(kernel, n, blocks, vals),
        out_shape=(
            jax.ShapeDtypeStruct((blocks, BLOCK), f32),
            jax.ShapeDtypeStruct((vals, BLOCK), f32),
            jax.ShapeDtypeStruct((rows, half), bf16),
            jax.ShapeDtypeStruct((share, width), f32),
        ),
        in_specs=[vmem, vmem, vmem, vmem],
        out_specs=(vmem, vmem, vmem, vmem),
        scratch_shapes=[
            pltpu.VMEM((2 * blocks, BLOCK, BLOCK), f32),
            pltpu.VMEM((2 * blocks, BLOCK, BLOCK), bf16),
            pltpu.VMEM((2 * blocks, BLOCK, width), bf16),
            pltpu.VMEM((vals, 1, BLOCK), f32),
            pltpu.VMEM((vals, 1, BLOCK), f32),
            pltpu.VMEM((rows, LANES), f32),
            pltpu.VMEM((rows, LANES), f32),
            pltpu.VMEM((2 * blocks, 1, BLOCK), f32),
            pltpu.VMEM((2 * blocks, 1, BLOCK), f32),
            pltpu.VMEM((2 * blocks, 1, BLOCK), f32),
            pltpu.VMEM((ITERS, 2, 2 * blocks, BLOCK), f32),
            pltpu.VMEM((ITERS, n, 2 * vals, BLOCK), f32),
            pltpu.VMEM((pairs, share, width), f32),
            pltpu.VMEM((pairs, share, width), f32),
            pltpu.VMEM((pairs, share, width), f32),
            pltpu.VMEM((pairs, share, width), f32),
            pltpu.VMEM((blocks, BLOCK, half), f32),
            pltpu.VMEM((blocks, BLOCK, half), f32),
            dma((ITERS,)), dma((ITERS,)),
            dma((ITERS, n)), dma((ITERS, n)),
            dma((pairs,)), dma((pairs,)),
            dma((pairs,)), dma((pairs,)),
            dma((blocks,)), dma((blocks,)),
        ],
        compiler_params=pltpu.CompilerParams(
            collective_id=0, has_side_effects=True, vmem_limit_bytes=56 * 1024 * 1024
        ),
    )(
        jnp.broadcast_to(tiles.reshape(-1, 1, 1), (2 * blocks, 1, BLOCK)),
        jnp.broadcast_to(counts.reshape(-1, 1, 1), (blocks, 1, BLOCK)),
        train_emb, val_emb.reshape(val_rows, width),
    )
    return (pot_train.reshape(-1), pot_val.reshape(1, -1), grad_train, grad_val[None])


def solution(mesh):
    return jax.shard_map(
        body,
        mesh=mesh,
        in_specs=(
            P(("groups", "rows"), None),
            P(("groups", "cols"), None, None),
            P(("groups", "rows"), "cols", None),
            P(("groups", "rows")),
        ),
        out_specs=(
            P(("groups", "rows")),
            P(("groups", "cols"), None),
            P(("groups", "rows"), "cols"),
            P(("groups", "cols"), "rows", None),
        ),
        check_vma=False,
    )
```

time: 461 us -> 153 us (0.33)
  waiting for transfers between devices: 200 us -> 0 us
  Pallas kernels: 0 us -> 143 us
  blocking collectives: 119 us -> 0 us
  other arithmetic: 63.6 us -> 0 us
  matrix products: 43.7 us -> 0 us
  between operations: 15.8 us -> 0.65 us
  local copies, waits for them, and re-layouts: 15.4 us -> 9.12 us
    psum x1 -> x0, waiting for transfers between devices: 200 us -> none  [body(): summed = lax.psum(val_terms, 'rows')]
    pallas_call x0 -> x1, Pallas kernels: none -> 143 us  [body(): pl.pallas_call(functools.partial(kernel, n, blocks, vals), out_shape=(jax...]
    pmax x6 -> x0, blocking collectives: 69.1 us -> none  [the longest x3 46.9 us: merge_val(): joined = lax.pmax(val_top, 'rows')]
    psum x6 -> x0, blocking collectives: 49.6 us -> none  [the longest x3 42 us: merge_val(): return (joined, lax.psum(val_sum * jnp.exp(val_top - joined), 'rows'))]
    dot_general x7 -> x0, matrix products: 43.7 us -> none  [the longest x1 16 us: body(): jnp.einsum('tkv,tkjd->vjd', block_hot, pushed, precision=lax.Precision.HI...]
    reduce_sum x9 -> x0, other arithmetic: 34.9 us -> none  [the longest x3 13.9 us: body(): jnp.sum(jnp.exp(back_scores - val_top[picked][:, :, None, :]), axis=2)]
    reduce_max x8 -> x0, other arithmetic: 21.9 us -> none  [the longest x3 13.7 us: body(): tile_top = jnp.max(back_scores, axis=2)]
    gather x17 -> x0, local copies, waits for them, and re-layouts: 10 us -> none  [the longest x1 5.42 us: body(): chosen = val_blocks[picked]]
  transfers between devices with their start and end apart: 2 -> 0, of which waited for: 1 -> 0; matrix products, arithmetic and copies ran while one was open for 4% -> 0% of each run, Pallas kernels for 0% -> 0%
where the time goes in v1:
time: 153 us
  Pallas kernels  143 us (93%)
  local copies, waits for them, and re-layouts  9.12 us (6%)
    pallas_call x1, Pallas kernels, body(): pl.pallas_call(functools.partial(kernel, n, blocks, vals), out_shape=(jax...  143 us
    unnamed x7, local copies, waits for them, and re-layouts  7.03 us

profile of v1, /device:TPU:11, one launch (start us, length us, event | category | flops | bytes accessed | tf_op | source)
XLA Modules:
  0.0 152.8 jit_solution(3864174311229437582)
XLA Ops:
  0.6 0.8 copy.9
  1.4 0.1 broadcast_in_dim.15
  1.5 1.3 broadcast_in_dim.17.counts_ref
  2.8 0.7 broadcast_in_dim.16.tiles_ref
  3.5 143.1 %shard_map.75 = (f32[4,512]{1,0:T(4,128)}, f32[4,512]{1,0:T(4,128)}, bf16[2048,384]{1,0:T(8,128)(2,1)}, f32[256,768]{1,0:T(8,128)}) custom-call(s32[8,1,512]{2,1,0:T(1,128)} %broadcast_in_dim.16.tiles_ref, s32[4,1,512]{2,1,0:T(1,128)} %broadcast_in_dim.17.counts_ref, bf16[2048,768]{1,0:T(8,128)(2,1)} %x_ref.1, bf16[2048,768]{1,0:T(8,128)(2,1)} %bitcast.9), custom_call_target="tpu_custom_call" | custom-call | tf_op jit(solution)/shard_map/pallas_call | solution.py:359
  146.5 0.0 copy-start
  146.6 1.4 copy.10
  147.9 1.3 copy.11
  149.2 2.7 %copy.14 = bf16[2048,384]{1,0:T(8,128)(2,1)} copy(bf16[2048,384]{1,0:T(8,128)(2,1)} %get-tuple-element.18) | data formatting | bytes 3145728
  151.9 0.0 copy-done
  151.9 0.9 copy.15
Async XLA Ops:
  146.5 5.4 %copy-start = (f32[256,768]{1,0:T(8,128)S(1)}, f32[256,768]{1,0:T(8,128)}, u32[]{:S(2)}) copy-start(f32[256,768]{1,0:T(8,128)} %get-tuple-element.11) | copy-start | bytes 2359300

commit v2 on v1

--- a/solution.py
+++ b/solution.py
@@ -16,6 +16,7 @@
 FLOOR = -1e30
 MESH = pl.DeviceIdType.MESH
 STRIPS = BLOCK // LANES
+PIECES = 2
 
 
 def strip(index):
@@ -45,9 +46,10 @@
     tiles_ref, counts_ref, x_ref, y_ref,
     pot_train_ref, pot_val_ref, grad_train_ref, grad_val_ref,
     cost, plan, chosen, val_sq, g_ref, f_wide, mass_wide, tile_top, tile_sum, row_part,
-    row_box, val_box, away, home, paired, landed, term_out, term_in,
+    row_box, val_box, parts_sum, paired, landed, term_out, term_in,
+    mate_in, core_in, mate_x, mate_tiles, mate_f, f_keep,
     row_send, row_recv, val_send, val_recv, pair_send, pair_recv, own_send, own_recv,
-    term_send, term_recv,
+    term_send, term_recv, mate_send, mate_recv, core_send, core_recv, small_send, small_recv,
 ):
     me = lax.axis_index("rows")
     core = lax.axis_index("cols")
@@ -56,11 +58,15 @@
     half_width = width // 2
     live_total = blocks * n * (3 * BLOCK // 4)
     val_total = vals * BLOCK * 2
-    pairs = n // 2
+    quads = n // 4
     share = vals * BLOCK // n
-    stage = lax.div(me, 2)
+    piece = share // PIECES
+    span_width = 2 * share
+    quad = lax.div(me, 4)
+    part = lax.rem(lax.div(me, 2), 2)
     side = lax.rem(me, 2)
-    mate = stage * 2 + 1 - side
+    mate = quad * 4 + (1 - part) * 2 + side
+    twin = quad * 4 + part * 2 + 1 - side
 
     barrier = pltpu.get_barrier_semaphore()
 
@@ -84,6 +90,38 @@
 
     def block_rows(index):
         return pl.ds(pl.multiple_of(index * BLOCK, BLOCK), BLOCK)
+
+    def mate_copy(t):
+        return pltpu.make_async_remote_copy(
+            src_ref=term_out.at[t], dst_ref=mate_in.at[t],
+            send_sem=mate_send.at[t], recv_sem=mate_recv.at[t],
+            device_id={"rows": mate}, device_id_type=MESH,
+        )
+
+    def core_copy(t):
+        return pltpu.make_async_remote_copy(
+            src_ref=mate_in.at[t], dst_ref=core_in.at[t],
+            send_sem=core_send.at[t], recv_sem=core_recv.at[t],
+            device_id={"cols": other}, device_id_type=MESH,
+        )
+
+    def small_copy(index, source, target):
+        return pltpu.make_async_remote_copy(
+            src_ref=source, dst_ref=target,
+            send_sem=small_send.at[index], recv_sem=small_recv.at[index],
+            device_id={"rows": mate}, device_id_type=MESH,
+        )
+
+    def half_of(which):
+        return pl.ds(pl.multiple_of(which * half_width, LANES), half_width)
+
+    tile_copy = small_copy(0, tiles_ref, mate_tiles)
+    tile_copy.start()
+
+    @pl.loop(0, blocks)
+    def _(t):
+        term_out[t] = x_ref[block_rows(t), half_of(core)].astype(jnp.float32)
+        mate_copy(t).start()
 
     for v in range(vals):
         for c in range(STRIPS):
@@ -158,6 +196,7 @@
             live = lane < counts_ref[t]
             pot_train_ref[t : t + 1, :] = jnp.where(live, f_all[t : t + 1] * (1.0 / SCALE), 0.0)
             f = jnp.where(live, f_all[t : t + 1], FLOOR)
+            f_keep[t : t + 1, :] = f
             for c in range(STRIPS):
                 f_wide[pl.ds(t * BLOCK + c * LANES, LANES), :] = jnp.broadcast_to(
                     to_column(f[:, c * LANES : (c + 1) * LANES]), (LANES, LANES)
@@ -202,6 +241,11 @@
         pot_val_ref[...] = g * (1.0 / SCALE)
         for v in range(vals):
             g_ref[v] = g[v : v + 1]
+        mate_copy(it).wait_recv()
+        core_copy(it).start()
+
+    f_copy = small_copy(1, f_keep, mate_f)
+    f_copy.start()
 
     @pl.loop(0, blocks)
     def _(t):
@@ -220,19 +264,24 @@
                 jnp.broadcast_to(jnp.sum(total, axis=1, keepdims=True), (LANES, LANES))
             )
 
-    def pair_copy(s):
-        return pltpu.make_async_remote_copy(
-            src_ref=away.at[s], dst_ref=paired.at[s],
-            send_sem=pair_send.at[s], recv_sem=pair_recv.at[s],
-            device_id={"rows": mate}, device_id_type=MESH,
-        )
-
-    def own_copy(s, slot):
-        goal = lax.rem(stage + 1 + s, pairs)
-        return pltpu.make_async_remote_copy(
-            src_ref=home.at[s], dst_ref=landed.at[slot],
-            send_sem=own_send.at[s], recv_sem=own_recv.at[slot],
-            device_id={"rows": goal * 2 + side}, device_id_type=MESH,
+    def rows_of_piece(j):
+        return pl.ds(pl.multiple_of(j * piece, piece), piece)
+
+    def pair_copy(s, j):
+        return pltpu.make_async_remote_copy(
+            src_ref=parts_sum.at[s, 1 - side, rows_of_piece(j)],
+            dst_ref=paired.at[s, rows_of_piece(j)],
+            send_sem=pair_send.at[s, j], recv_sem=pair_recv.at[s, j],
+            device_id={"rows": twin}, device_id_type=MESH,
+        )
+
+    def own_copy(s, slot, j):
+        goal = lax.rem(quad + 1 + s, quads)
+        return pltpu.make_async_remote_copy(
+            src_ref=parts_sum.at[s, side, rows_of_piece(j)],
+            dst_ref=landed.at[slot, rows_of_piece(j)],
+            send_sem=own_send.at[s, j], recv_sem=own_recv.at[slot, j],
+            device_id={"rows": goal * 4 + part * 2 + side}, device_id_type=MESH,
         )
 
     def term_copy(t):
@@ -242,54 +291,12 @@
             device_id={"cols": other}, device_id_type=MESH,
         )
 
-    @pl.loop(0, pairs)
-    def _(s):
-        goal = lax.rem(stage + 1 + s, pairs)
-
-        def push(which):
-            start = (goal * 2 + which) * share
-            v = lax.div(start, BLOCK)
-            inside = lax.rem(start, BLOCK)
-            total = jnp.zeros((share, width), jnp.float32)
-            for t in range(blocks):
-                if share % LANES == 0:
-                    span = pl.ds(pl.multiple_of(inside, share), share)
-                    parts = [plan[t * 2 + k, :, span] for k in range(2)]
-                    offset = None
-                else:
-                    base = lax.div(inside, LANES) * LANES
-                    span = pl.ds(pl.multiple_of(base, LANES), LANES)
-                    parts = [plan[t * 2 + k, :, span] for k in range(2)]
-                    offset = inside - base
-                zero = jnp.zeros_like(parts[0])
-                picked = jnp.where(
-                    tiles_ref[t * 2][:, 0 : zero.shape[1]] == v, parts[0],
-                    jnp.where(tiles_ref[t * 2 + 1][:, 0 : zero.shape[1]] == v, parts[1], zero),
-                )
-                product = lax.dot_general(
-                    picked, x_ref[t * BLOCK : (t + 1) * BLOCK, :], (((0,), (0,)), ((), ())),
-                    preferred_element_type=jnp.float32,
-                )
-                if offset is not None:
-                    keep = product[0:share]
-                    for piece in range(1, LANES // share):
-                        keep = jnp.where(
-                            offset == piece * share, product[piece * share : (piece + 1) * share], keep
-                        )
-                    product = keep
-                total = total + product
-            return total
-
-        away[s] = push(1 - side)
-        pair_copy(s).start()
-        home[s] = push(side)
-
     @pl.loop(0, blocks)
     def _(t):
         mass = mass_wide[block_rows(t), 0:1]
 
         def pull(which):
-            span = pl.ds(pl.multiple_of(which * half_width, LANES), half_width)
+            span = half_of(which)
             total = mass * x_ref[block_rows(t), span].astype(jnp.float32)
             pulled = sum(
                 jnp.dot(
@@ -300,9 +307,85 @@
             )
             return total - pulled
 
+        mate_copy(t).wait_send()
         term_out[t] = pull(other)
         term_copy(t).start()
         cost[t, :, 0:half_width] = pull(core)
+
+    tile_copy.wait()
+    f_copy.wait()
+    for t in range(blocks):
+        for c in range(STRIPS):
+            f_wide[pl.ds(t * BLOCK + c * LANES, LANES), :] = jnp.broadcast_to(
+                to_column(mate_f[t : t + 1, strip(c)]), (LANES, LANES)
+            )
+
+    @pl.loop(ITERS, blocks)
+    def _(t):
+        mate_copy(t).wait_recv()
+        core_copy(t).start()
+
+    @pl.loop(0, blocks)
+    def _(t):
+        core_copy(t).wait()
+        mate_x[block_rows(t), half_of(core)] = mate_in[t].astype(jnp.bfloat16)
+        mate_x[block_rows(t), half_of(other)] = core_in[t].astype(jnp.bfloat16)
+
+    @pl.loop(0, quads)
+    def _(s):
+        goal = lax.rem(quad + 1 + s, quads)
+        start = (goal * 4 + part * 2) * share
+        v = lax.div(start, BLOCK)
+        span = pl.ds(pl.multiple_of(lax.rem(start, BLOCK), span_width), span_width)
+        y = y_ref[pl.ds(pl.multiple_of(start, span_width), span_width), :]
+        y_sq = val_sq[v, :, span]
+        g = g_ref[v, :, span]
+        parts_sum[s] = jnp.zeros((2, share, width), jnp.float32)
+
+        @pl.loop(0, blocks)
+        def _(t):
+            first = plan[t * 2, :, span]
+            second = plan[t * 2 + 1, :, span]
+            own = jnp.where(
+                tiles_ref[t * 2][:, 0:span_width] == v, first,
+                jnp.where(tiles_ref[t * 2 + 1][:, 0:span_width] == v, second, jnp.zeros_like(first)),
+            )
+            total = lax.dot_general(
+                own, x_ref[block_rows(t), :], (((0,), (0,)), ((), ())),
+                preferred_element_type=jnp.float32,
+            )
+            x = mate_x[block_rows(t), :]
+            xf = x.astype(jnp.float32)
+            x_sq = jnp.sum(xf * xf, axis=1, keepdims=True)
+            inner = lax.dot_general(
+                x, y, (((1,), (1,)), ((), ())), preferred_element_type=jnp.float32
+            )
+            met = jnp.logical_or(
+                mate_tiles[t * 2][:, 0:span_width] == v, mate_tiles[t * 2 + 1][:, 0:span_width] == v
+            )
+            value = jnp.exp2(
+                f_wide[block_rows(t), 0:1] + jnp.where(met, g, FLOOR)
+                - ((x_sq + y_sq) - 2.0 * inner) * SCALE
+            )
+            total = total + lax.dot_general(
+                value.astype(jnp.bfloat16), x, (((0,), (0,)), ((), ())),
+                preferred_element_type=jnp.float32,
+            )
+            parts_sum[s, 0] = parts_sum[s, 0] + total[0:share]
+            parts_sum[s, 1] = parts_sum[s, 1] + total[share:]
+
+        @pl.loop(0, PIECES)
+        def _(j):
+            pair_copy(s, j).start()
+
+    @pl.loop(0, quads - 1)
+    def _(s):
+        @pl.loop(0, PIECES)
+        def _(j):
+            pair_copy(s, j).wait_recv()
+            at = rows_of_piece(j)
+            parts_sum[s, side, at] = parts_sum[s, side, at] + paired[s, at]
+            own_copy(s, quad, j).start()
 
     @pl.loop(0, blocks)
     def _(t):
@@ -311,31 +394,34 @@
             live_total * 2.0 * (cost[t, :, 0:half_width] + term_in[t])
         ).astype(jnp.bfloat16)
 
-    @pl.loop(0, pairs - 1)
+    @pl.loop(0, PIECES)
+    def _(j):
+        pair_copy(quads - 1, j).wait_recv()
+
+    own_rows = y_ref[pl.ds(pl.multiple_of(me * share, share), share), :].astype(jnp.float32)
+    grad_val_ref[...] = parts_sum[quads - 1, side] + paired[quads - 1]
+
+    @pl.loop(0, quads - 1)
     def _(s):
-        pair_copy(s).wait_recv()
-        home[s] = home[s] + paired[s]
-        own_copy(s, stage).start()
-
-    pair_copy(pairs - 1).wait_recv()
-    home[pairs - 1] = home[pairs - 1] + paired[pairs - 1]
-
-    @pl.loop(0, pairs - 1)
-    def _(s):
-        slot = lax.rem(stage + 1 + s, pairs)
-        own_copy(s, slot).wait_recv()
-        home[pairs - 1] = home[pairs - 1] + landed[slot]
-
-    own_rows = y_ref[pl.ds(pl.multiple_of(me * share, share), share), :].astype(jnp.float32)
-    grad_val_ref[...] = 2.0 * (own_rows - val_total * home[pairs - 1])
-
-    @pl.loop(0, pairs)
-    def _(s):
-        pair_copy(s).wait_send()
-
-    @pl.loop(0, pairs - 1)
-    def _(s):
-        own_copy(s, stage).wait_send()
+        slot = lax.rem(quad + 1 + s, quads)
+
+        @pl.loop(0, PIECES)
+        def _(j):
+            own_copy(s, slot, j).wait_recv()
+
+        grad_val_ref[...] = grad_val_ref[...] + landed[slot]
+
+    grad_val_ref[...] = 2.0 * (own_rows - val_total * grad_val_ref[...])
+
+    @pl.loop(0, PIECES)
+    def _(j):
+        @pl.loop(0, quads)
+        def _(s):
+            pair_copy(s, j).wait_send()
+
+        @pl.loop(0, quads - 1)
+        def _(s):
+            own_copy(s, quad, j).wait_send()
 
     @pl.loop(0, ITERS)
     def _(it):
@@ -351,7 +437,7 @@
     val_rows = val_emb.shape[1]
     vals = val_rows // BLOCK
     share = val_rows // n
-    pairs = n // 2
+    quads = n // 4
     half = width // 2
     f32, bf16 = jnp.float32, jnp.bfloat16
     dma = pltpu.SemaphoreType.DMA
@@ -379,20 +465,28 @@
             pltpu.VMEM((2 * blocks, 1, BLOCK), f32),
             pltpu.VMEM((ITERS, 2, 2 * blocks, BLOCK), f32),
             pltpu.VMEM((ITERS, n, 2 * vals, BLOCK), f32),
-            pltpu.VMEM((pairs, share, width), f32),
-            pltpu.VMEM((pairs, share, width), f32),
-            pltpu.VMEM((pairs, share, width), f32),
-            pltpu.VMEM((pairs, share, width), f32),
+            pltpu.VMEM((quads, 2, share, width), f32),
+            pltpu.VMEM((quads, share, width), f32),
+            pltpu.VMEM((quads, share, width), f32),
             pltpu.VMEM((blocks, BLOCK, half), f32),
             pltpu.VMEM((blocks, BLOCK, half), f32),
+            pltpu.VMEM((blocks, BLOCK, half), f32),
+            pltpu.VMEM((blocks, BLOCK, half), f32),
+            pltpu.VMEM((rows, width), bf16),
+            pltpu.VMEM((2 * blocks, 1, BLOCK), jnp.int32),
+            pltpu.VMEM((blocks, BLOCK), f32),
+            pltpu.VMEM((blocks, BLOCK), f32),
             dma((ITERS,)), dma((ITERS,)),
             dma((ITERS, n)), dma((ITERS, n)),
-            dma((pairs,)), dma((pairs,)),
-            dma((pairs,)), dma((pairs,)),
+            dma((quads, PIECES)), dma((quads, PIECES)),
+            dma((quads, PIECES)), dma((quads, PIECES)),
             dma((blocks,)), dma((blocks,)),
+            dma((blocks,)), dma((blocks,)),
+            dma((blocks,)), dma((blocks,)),
+            dma((2,)), dma((2,)),
         ],
         compiler_params=pltpu.CompilerParams(
-            collective_id=0, has_side_effects=True, vmem_limit_bytes=56 * 1024 * 1024
+            collective_id=0, has_side_effects=True, vmem_limit_bytes=60 * 1024 * 1024
         ),
     )(
         jnp.broadcast_to(tiles.reshape(-1, 1, 1), (2 * blocks, 1, BLOCK)),

time: 153 us -> 180 us (1.18)
  the two profiles are of different devices: /device:TPU:11 before, /device:TPU:0 now
where the time goes in v2:
time: 180 us
  Pallas kernels  170 us (94%)
  local copies, waits for them, and re-layouts  9.12 us (5%)
    pallas_call x1, Pallas kernels, body(): pl.pallas_call(functools.partial(kernel, n, blocks, vals), out_shape=(jax...  170 us
    unnamed x7, local copies, waits for them, and re-layouts  7.03 us

profile of v2, /device:TPU:0, one launch (start us, length us, event | category | flops | bytes accessed | tf_op | source)
XLA Modules:
  0.0 179.7 jit_solution(13269064208085269385)
XLA Ops:
  0.6 0.8 copy.9
  1.4 0.1 broadcast_in_dim.15
  1.5 1.3 broadcast_in_dim.17.counts_ref
  2.8 0.7 broadcast_in_dim.16.tiles_ref
  3.5 169.9 %shard_map.75 = (f32[4,512]{1,0:T(4,128)}, f32[4,512]{1,0:T(4,128)}, bf16[2048,384]{1,0:T(8,128)(2,1)}, f32[256,768]{1,0:T(8,128)}) custom-call(s32[8,1,512]{2,1,0:T(1,128)} %broadcast_in_dim.16.tiles_ref, s32[4,1,512]{2,1,0:T(1,128)} %broadcast_in_dim.17.counts_ref, bf16[2048,768]{1,0:T(8,128)(2,1)} %x_ref.1, bf16[2048,768]{1,0:T(8,128)(2,1)} %bitcast.9), custom_call_target="tpu_custom_call" | custom-call | tf_op jit(solution)/shard_map/pallas_call | solution.py:445
  173.4 0.0 copy-start
  173.5 1.4 copy.10
  174.8 1.3 copy.11
  176.1 2.7 %copy.14 = bf16[2048,384]{1,0:T(8,128)(2,1)} copy(bf16[2048,384]{1,0:T(8,128)(2,1)} %get-tuple-element.18) | data formatting | bytes 3145728
  178.8 0.0 copy-done
  178.8 0.9 copy.15
Async XLA Ops:
  173.4 5.4 %copy-start = (f32[256,768]{1,0:T(8,128)S(1)}, f32[256,768]{1,0:T(8,128)}, u32[]{:S(2)}) copy-start(f32[256,768]{1,0:T(8,128)} %get-tuple-element.11) | copy-start | bytes 2359300

commit v3 on v1

--- a/solution.py
+++ b/solution.py
@@ -16,6 +16,7 @@
 FLOOR = -1e30
 MESH = pl.DeviceIdType.MESH
 STRIPS = BLOCK // LANES
+PIECES = 4
 
 
 def strip(index):
@@ -220,20 +221,35 @@
                 jnp.broadcast_to(jnp.sum(total, axis=1, keepdims=True), (LANES, LANES))
             )
 
-    def pair_copy(s):
+    piece = share // PIECES
+
+    def rows_of(j):
+        return pl.ds(pl.multiple_of(j * piece, piece), piece)
+
+    def pair_copy(s, j):
         return pltpu.make_async_remote_copy(
-            src_ref=away.at[s], dst_ref=paired.at[s],
-            send_sem=pair_send.at[s], recv_sem=pair_recv.at[s],
+            src_ref=away.at[s, rows_of(j)], dst_ref=paired.at[s, rows_of(j)],
+            send_sem=pair_send.at[s, j], recv_sem=pair_recv.at[s, j],
             device_id={"rows": mate}, device_id_type=MESH,
         )
 
-    def own_copy(s, slot):
+    def own_copy(s, slot, j):
         goal = lax.rem(stage + 1 + s, pairs)
         return pltpu.make_async_remote_copy(
-            src_ref=home.at[s], dst_ref=landed.at[slot],
-            send_sem=own_send.at[s], recv_sem=own_recv.at[slot],
+            src_ref=home.at[s, rows_of(j)], dst_ref=landed.at[slot, rows_of(j)],
+            send_sem=own_send.at[s, j], recv_sem=own_recv.at[slot, j],
             device_id={"rows": goal * 2 + side}, device_id_type=MESH,
         )
+
+    def merge_piece(s, j):
+        pair_copy(s, j).wait_recv()
+        home[s, rows_of(j)] = home[s, rows_of(j)] + paired[s, rows_of(j)]
+
+    def relay(s):
+        @pl.loop(0, PIECES)
+        def _(j):
+            merge_piece(s, j)
+            own_copy(s, stage, j).start()
 
     def term_copy(t):
         return pltpu.make_async_remote_copy(
@@ -281,8 +297,14 @@
             return total
 
         away[s] = push(1 - side)
-        pair_copy(s).start()
+
+        @pl.loop(0, PIECES)
+        def _(j):
+            pair_copy(s, j).start()
+
         home[s] = push(side)
+
+    relay(0)
 
     @pl.loop(0, blocks)
     def _(t):
@@ -304,6 +326,10 @@
         term_copy(t).start()
         cost[t, :, 0:half_width] = pull(core)
 
+    @pl.loop(1, pairs - 1)
+    def _(s):
+        relay(s)
+
     @pl.loop(0, blocks)
     def _(t):
         term_copy(t).wait()
@@ -311,31 +337,32 @@
             live_total * 2.0 * (cost[t, :, 0:half_width] + term_in[t])
         ).astype(jnp.bfloat16)
 
-    @pl.loop(0, pairs - 1)
-    def _(s):
-        pair_copy(s).wait_recv()
-        home[s] = home[s] + paired[s]
-        own_copy(s, stage).start()
-
-    pair_copy(pairs - 1).wait_recv()
-    home[pairs - 1] = home[pairs - 1] + paired[pairs - 1]
+    @pl.loop(0, PIECES)
+    def _(j):
+        merge_piece(pairs - 1, j)
 
     @pl.loop(0, pairs - 1)
     def _(s):
         slot = lax.rem(stage + 1 + s, pairs)
-        own_copy(s, slot).wait_recv()
+
+        @pl.loop(0, PIECES)
+        def _(j):
+            own_copy(s, slot, j).wait_recv()
+
         home[pairs - 1] = home[pairs - 1] + landed[slot]
 
     own_rows = y_ref[pl.ds(pl.multiple_of(me * share, share), share), :].astype(jnp.float32)
     grad_val_ref[...] = 2.0 * (own_rows - val_total * home[pairs - 1])
 
-    @pl.loop(0, pairs)
-    def _(s):
-        pair_copy(s).wait_send()
-
-    @pl.loop(0, pairs - 1)
-    def _(s):
-        own_copy(s, stage).wait_send()
+    @pl.loop(0, PIECES)
+    def _(j):
+        @pl.loop(0, pairs)
+        def _(s):
+            pair_copy(s, j).wait_send()
+
+        @pl.loop(0, pairs - 1)
+        def _(s):
+            own_copy(s, stage, j).wait_send()
 
     @pl.loop(0, ITERS)
     def _(it):
@@ -387,8 +414,8 @@
             pltpu.VMEM((blocks, BLOCK, half), f32),
             dma((ITERS,)), dma((ITERS,)),
             dma((ITERS, n)), dma((ITERS, n)),
-            dma((pairs,)), dma((pairs,)),
-            dma((pairs,)), dma((pairs,)),
+            dma((pairs, PIECES)), dma((pairs, PIECES)),
+            dma((pairs, PIECES)), dma((pairs, PIECES)),
             dma((blocks,)), dma((blocks,)),
         ],
         compiler_params=pltpu.CompilerParams(

time: 153 us -> 146 us (0.954)
  Pallas kernels: 143 us -> 136 us
    pallas_call x1, Pallas kernels: 143 us -> 136 us  [body(): pl.pallas_call(functools.partial(kernel, n, blocks, vals), out_shape=(jax...]
where the time goes in v3:
time: 146 us; the launch traced here: 145 us
  Pallas kernels  136 us (93%)
  local copies, waits for them, and re-layouts  9.12 us (6%)
    pallas_call x1, Pallas kernels, body(): pl.pallas_call(functools.partial(kernel, n, blocks, vals), out_shape=(jax...  136 us
    unnamed x7, local copies, waits for them, and re-layouts  7.03 us

profile of v3, /device:TPU:11, one launch (start us, length us, event | category | flops | bytes accessed | tf_op | source)
XLA Modules:
  0.0 145.4 jit_solution(3281146060977106452)
XLA Ops:
  0.6 0.8 copy.9
  1.4 0.1 broadcast_in_dim.15
  1.5 1.3 broadcast_in_dim.17.counts_ref
  2.8 0.7 broadcast_in_dim.16.tiles_ref
  3.5 135.6 %shard_map.75 = (f32[4,512]{1,0:T(4,128)}, f32[4,512]{1,0:T(4,128)}, bf16[2048,384]{1,0:T(8,128)(2,1)}, f32[256,768]{1,0:T(8,128)}) custom-call(s32[8,1,512]{2,1,0:T(1,128)} %broadcast_in_dim.16.tiles_ref, s32[4,1,512]{2,1,0:T(1,128)} %broadcast_in_dim.17.counts_ref, bf16[2048,768]{1,0:T(8,128)(2,1)} %x_ref.1, bf16[2048,768]{1,0:T(8,128)(2,1)} %bitcast.9), custom_call_target="tpu_custom_call" | custom-call | tf_op jit(solution)/shard_map/pallas_call | solution.py:386
  139.1 0.0 copy-start
  139.1 1.4 copy.10
  140.5 1.3 copy.11
  141.8 2.7 %copy.14 = bf16[2048,384]{1,0:T(8,128)(2,1)} copy(bf16[2048,384]{1,0:T(8,128)(2,1)} %get-tuple-element.18) | data formatting | bytes 3145728
  144.5 0.0 copy-done
  144.5 0.9 copy.15
Async XLA Ops:
  139.1 5.4 %copy-start = (f32[256,768]{1,0:T(8,128)S(1)}, f32[256,768]{1,0:T(8,128)}, u32[]{:S(2)}) copy-start(f32[256,768]{1,0:T(8,128)} %get-tuple-element.11) | copy-start | bytes 2359300

commit v4 on v3

--- a/solution.py
+++ b/solution.py
@@ -16,7 +16,7 @@
 FLOOR = -1e30
 MESH = pl.DeviceIdType.MESH
 STRIPS = BLOCK // LANES
-PIECES = 4
+PIECES = 8
 
 
 def strip(index):
@@ -43,7 +43,7 @@
 
 def kernel(
     n, blocks, vals,
-    tiles_ref, counts_ref, x_ref, y_ref,
+    tiles_ref, x_ref, y_ref,
     pot_train_ref, pot_val_ref, grad_train_ref, grad_val_ref,
     cost, plan, chosen, val_sq, g_ref, f_wide, mass_wide, tile_top, tile_sum, row_part,
     row_box, val_box, away, home, paired, landed, term_out, term_in,
@@ -156,7 +156,7 @@
         f_all = math.log2(1.0 / live_total) - (top + jnp.log2(total))
         lane = lax.broadcasted_iota(jnp.int32, (1, BLOCK), 1)
         for t in range(blocks):
-            live = lane < counts_ref[t]
+            live = lane < tiles_ref[2 * blocks + t]
             pot_train_ref[t : t + 1, :] = jnp.where(live, f_all[t : t + 1] * (1.0 / SCALE), 0.0)
             f = jnp.where(live, f_all[t : t + 1], FLOOR)
             for c in range(STRIPS):
@@ -383,6 +383,7 @@
     f32, bf16 = jnp.float32, jnp.bfloat16
     dma = pltpu.SemaphoreType.DMA
     vmem = pl.BlockSpec(memory_space=pltpu.VMEM)
+    small = jnp.concatenate([tiles.reshape(-1), counts])
     pot_train, pot_val, grad_train, grad_val = pl.pallas_call(
         functools.partial(kernel, n, blocks, vals),
         out_shape=(
@@ -391,7 +392,7 @@
             jax.ShapeDtypeStruct((rows, half), bf16),
             jax.ShapeDtypeStruct((share, width), f32),
         ),
-        in_specs=[vmem, vmem, vmem, vmem],
+        in_specs=[vmem, vmem, vmem],
         out_specs=(vmem, vmem, vmem, vmem),
         scratch_shapes=[
             pltpu.VMEM((2 * blocks, BLOCK, BLOCK), f32),
@@ -422,8 +423,7 @@
             collective_id=0, has_side_effects=True, vmem_limit_bytes=56 * 1024 * 1024
         ),
     )(
-        jnp.broadcast_to(tiles.reshape(-1, 1, 1), (2 * blocks, 1, BLOCK)),
-        jnp.broadcast_to(counts.reshape(-1, 1, 1), (blocks, 1, BLOCK)),
+        jnp.broadcast_to(small.reshape(-1, 1, 1), (3 * blocks, 1, BLOCK)),
         train_emb, val_emb.reshape(val_rows, width),
     )
     return (pot_train.reshape(-1), pot_val.reshape(1, -1), grad_train, grad_val[None])

time: 146 us -> 147 us (level)
  no operation moved by 1% of the time
where the time goes in v4:
time: 147 us; the launch traced here: 146 us
  Pallas kernels  137 us (93%)
  local copies, waits for them, and re-layouts  7.8 us (5%)
    pallas_call x1, Pallas kernels, body(): pl.pallas_call(functools.partial(kernel, n, blocks, vals), out_shape=(jax...  137 us
    unnamed x7, local copies, waits for them, and re-layouts  7.03 us

profile of v4, /device:TPU:11, one launch (start us, length us, event | category | flops | bytes accessed | tf_op | source)
XLA Modules:
  0.0 145.9 jit_solution(10002824665452392333)
XLA Ops:
  0.6 0.8 copy.9
  1.4 0.1 reshape.24
  1.5 0.7 pad_add_fusion
  2.2 0.7 broadcast_in_dim.8.tiles_ref
  2.9 136.7 %shard_map.75 = (f32[4,512]{1,0:T(4,128)}, f32[4,512]{1,0:T(4,128)}, bf16[2048,384]{1,0:T(8,128)(2,1)}, f32[256,768]{1,0:T(8,128)}) custom-call(s32[12,1,512]{2,1,0:T(1,128)} %broadcast_in_dim.8.tiles_ref, bf16[2048,768]{1,0:T(8,128)(2,1)} %x_ref.1, bf16[2048,768]{1,0:T(8,128)(2,1)} %bitcast.9), custom_call_target="tpu_custom_call" | custom-call | tf_op jit(solution)/shard_map/pallas_call | solution.py:387
  139.6 0.0 copy-start
  139.6 1.4 copy.10
  141.0 1.3 copy.11
  142.3 2.7 %copy.14 = bf16[2048,384]{1,0:T(8,128)(2,1)} copy(bf16[2048,384]{1,0:T(8,128)(2,1)} %get-tuple-element.18) | data formatting | bytes 3145728
  145.0 0.0 copy-done
  145.0 0.9 copy.15
Async XLA Ops:
  139.6 5.4 %copy-start = (f32[256,768]{1,0:T(8,128)S(1)}, f32[256,768]{1,0:T(8,128)}, u32[]{:S(2)}) copy-start(f32[256,768]{1,0:T(8,128)} %get-tuple-element.11) | copy-start | bytes 2359300
